TPU v7x, 1024 devices: a whole 4x8x16 slice. The times are simulated.
1024 devices in a mesh: group: 8 (over y), node: 64 (over x, z), tp: 2 (over core).
Axes of the slice: x: 4, y: 8, z: 16, core: 2. Of those that a mesh axis runs over, the one named last changes fastest.
Arguments:
- out_grad: bfloat16 [64, 64, 3584], P('node', 'group', 'tp'), may hold values from -6 to 6
- expert_ids: int32 [64, 64, 8], P('node'), may hold values from 0 to 127, all different within a row; in each aligned block of 64 rows (0 to 63, 64 to 127, ..., all dimensions but the last counted through in order) at most 8 rows name the same one
- gate_scores: bfloat16 [64, 64, 8], P('node'), may hold values from 0.099609375 to 0.59765625
- saved_gate: bfloat16 [512, 64, 8, 256], P(('group', 'node')), may hold values from -6 to 6
- saved_up: bfloat16 [512, 64, 8, 256], P(('group', 'node')), may hold values from -6 to 6
- w_gate: bfloat16 [512, 3584, 256], P(('group', 'node'), 'tp'), may hold values from -0.09375 to 0.09375
- w_up: bfloat16 [512, 3584, 256], P(('group', 'node'), 'tp'), may hold values from -0.09375 to 0.09375
- w_down: bfloat16 [512, 256, 3584], P(('group', 'node'), None, 'tp'), may hold values from -0.1875 to 0.1875
Outputs:
- input_grad: bfloat16 [64, 64, 3584], P('node', 'group', 'tp')
Inputs may be any that keep to these rules, and one draw needn't show every extreme that they name: Each row names 8 different experts; among the rows expert_ids[n, :, :] of one n no expert is named more than 8 times.
All inputs are finite; a program needn't handle non-finite values.
Results may differ from a plain program's by a relative error of at most 0.009.
Values may be sent and summed in bfloat16 or wider, within the bound.
A program may use at most 32 MiB of HBM per device.

v0:
```python
import jax
import jax.numpy as jnp
from jax import lax
from jax.sharding import PartitionSpec as P

FF = 1024


def per_device(out_grad, expert_ids, gate_scores, saved_gate, saved_up, w_gate, w_up, w_down):
    feature_half = out_grad.shape[2]
    hidden_dev = w_down.shape[1]
    node_count = lax.axis_size("node")
    slot_count = saved_gate.shape[2]
    spread = FF // hidden_dev
    experts_here = node_count // spread
    slots_all = node_count * slot_count
    group_index = lax.axis_index("group")
    relay_rows = lax.all_gather(out_grad, "group", axis=1, tiled=True)[0]
    row_count = relay_rows.shape[0]
    local_ids = expert_ids[0] - group_index * experts_here
    scores = gate_scores[0].astype(jnp.float32)
    hits = local_ids[:, :, None] == jnp.arange(experts_here, dtype=jnp.int32)[None, None, :]
    pick = jnp.sum(hits.astype(jnp.int32), axis=1)
    weight = jnp.sum(jnp.where(hits, scores[:, :, None], jnp.float32(0.0)), axis=1)
    slot_index = jnp.cumsum(pick, axis=0) - pick
    slot_range = jnp.arange(slot_count, dtype=jnp.int32)
    placing = (slot_index.T[:, None, :] == slot_range[None, :, None]) & (pick.T[:, None, :] > 0)
    placing_flat = placing.reshape(experts_here * slot_count, row_count)
    packed = jnp.dot(
        placing_flat.astype(jnp.bfloat16), relay_rows, preferred_element_type=jnp.float32
    ).astype(jnp.bfloat16)
    slot_weight = jnp.sum(placing.astype(jnp.float32) * weight.T[:, None, :], axis=2).astype(
        jnp.bfloat16
    )
    send_rows = jnp.repeat(packed.reshape(experts_here, slot_count, feature_half), spread, axis=0)
    send_weight = jnp.repeat(slot_weight, spread, axis=0)
    arrived, arrived_weight = (
        lax.all_to_all(send_rows, "node", split_axis=0, concat_axis=0, tiled=True),
        lax.all_to_all(send_weight, "node", split_axis=0, concat_axis=0, tiled=True),
    )
    flat_rows = arrived.reshape(slots_all, feature_half)
    partial_hidden = lax.dot_general(
        flat_rows, w_down[0], (((1,), (1,)), ((), ())), preferred_element_type=jnp.float32
    )
    hidden_grad = lax.psum(partial_hidden, "tp")
    gate_pre = saved_gate[0].reshape(slots_all, hidden_dev).astype(jnp.float32)
    up_pre = saved_up[0].reshape(slots_all, hidden_dev).astype(jnp.float32)
    scaled = arrived_weight.reshape(slots_all, 1).astype(jnp.float32) * hidden_grad
    sigmoid_gate = jax.nn.sigmoid(gate_pre)
    gate_grad = (scaled * up_pre * sigmoid_gate * (1.0 + gate_pre * (1.0 - sigmoid_gate))).astype(
        jnp.bfloat16
    )
    up_grad = (scaled * gate_pre * sigmoid_gate).astype(jnp.bfloat16)
    part_grad = lax.dot_general(
        gate_grad, w_gate[0], (((1,), (1,)), ((), ())), preferred_element_type=jnp.float32
    )
    part_grad = part_grad + lax.dot_general(
        up_grad, w_up[0], (((1,), (1,)), ((), ())), preferred_element_type=jnp.float32
    )
    part_grad = part_grad.astype(jnp.bfloat16).reshape(node_count, slot_count, feature_half)
    returned = lax.all_to_all(part_grad, "node", split_axis=0, concat_axis=0, tiled=True)
    summed = jnp.sum(
        returned.reshape(experts_here, spread, slot_count, feature_half).astype(jnp.float32), axis=1
    )
    summed = summed.reshape(experts_here * slot_count, feature_half)
    token_grad = lax.dot_general(
        placing_flat.astype(jnp.float32),
        summed,
        (((0,), (0,)), ((), ())),
        precision=lax.Precision.HIGHEST,
        preferred_element_type=jnp.float32,
    )
    own_grad = lax.psum_scatter(token_grad, "group", scatter_dimension=0, tiled=True)
    return own_grad.astype(jnp.bfloat16)[None]


def solution(mesh):
    placed = (
        P("node", "group", "tp"),
        P("node", None, None),
        P("node", None, None),
        P(("group", "node"), None, None, None),
        P(("group", "node"), None, None, None),
        P(("group", "node"), "tp", None),
        P(("group", "node"), "tp", None),
        P(("group", "node"), None, "tp"),
    )
    return jax.shard_map(
        per_device, mesh=mesh, in_specs=placed, out_specs=P("node", "group", "tp"), check_vma=False
    )
```

profile of v0, /device:TPU:6, one launch (start us, length us, event | category | flops | bytes accessed | tf_op | source)
XLA Modules:
  0.0 330.2 jit_solution(6665756667420105660)
XLA Ops:
  6.5 0.0 copy-start
  6.5 0.0 all-reduce.2.cloned.1.call-start
  6.5 0.8 subtract_bitcast_fusion.1
  7.3 0.1 copy.27
  7.4 0.1 reduce_window_sum.11
  7.5 0.1 copy.29
  7.6 26.5 %all_gather.3 = bf16[1,64,1792]{2,1,0:T(8,128)(2,1)S(1)} all-gather(bf16[1,8,1792]{2,1,0:T(8,128)(2,1)} %param.8), channel_id=1, replica_groups=mesh['group'=8,'node'=64,'tp'=2] {'group'}, dimensions={1}, use_global_device_ids=true | all-gather | bytes 258048 | tf_op jit(solution)/shard_map/all_gather | solution.py:18
  34.1 0.3 fusion.1
  34.4 0.1 broadcast_in_dim.31
  34.5 0.0 copy-start.6
  34.5 100.4 %all_to_all.19 = bf16[64,8,1792]{2,1,0:T(8,128)(2,1)S(1)} all-to-all(bf16[64,8,1792]{2,1,0:T(8,128)(2,1)S(1)} %bitcast.58), channel_id=1, replica_groups=mesh['group'=8,'node'=64,'tp'=2] {'node'}, dimensions={0} | all-to-all | bytes 3670016 | tf_op jit(solution)/shard_map/all_to_all | solution.py:38
  135.0 0.0 copy-done.6
  135.0 0.0 copy-start.5
  135.0 0.0 copy-start.2
  135.0 0.0 copy-start.4
  135.0 1.5 fusion.2
  136.5 0.0 all-reduce.2.cloned.1.call-update
  136.5 0.0 reduce-scatter.2.cloned.1.call-start
  136.5 0.0 copy-done.5
  136.6 0.1 select_reduce_fusion
  136.7 22.7 %all_to_all.20 = bf16[64,1,8]{2,1,0:T(2,128)(2,1)S(1)} all-to-all(bf16[64,1,8]{2,1,0:T(2,128)(2,1)S(1)} %copy.30), channel_id=1, replica_groups=mesh['group'=8,'node'=64,'tp'=2] {'node'}, dimensions={0} | all-to-all | bytes 2048 | tf_op jit(solution)/shard_map/all_to_all | solution.py:39
  159.4 0.1 convert_reduce_fusion.2
  159.5 0.1 reshape.95
  159.6 0.0 copy-start.3
  159.6 17.0 %all-reduce.2.cloned.1.call-done = f32[512,256]{1,0:T(8,128)} async-done(((f32[512,256]{1,0:T(8,128)}), f32[512,256]{1,0:T(8,128)}) %all-reduce.2.cloned.1.call-update) | async-done | bytes 524304 | tf_op jit(solution)/shard_map/psum | solution.py:45
  176.6 0.0 copy-done
  176.6 0.0 copy-done.2
  176.6 0.0 copy-done.4
  176.6 0.0 copy-start.1
  176.6 1.9 fusion.5
  178.6 0.0 copy-done.3
  178.6 0.0 copy-done.1
  178.6 0.8 fusion
  179.4 102.4 %all_to_all.21 = bf16[64,8,1792]{2,1,0:T(8,128)(2,1)S(1)} all-to-all(bf16[64,8,1792]{2,1,0:T(8,128)(2,1)S(1)} %fusion), channel_id=1, replica_groups=mesh['group'=8,'node'=64,'tp'=2] {'node'}, dimensions={0} | all-to-all | bytes 3670016 | tf_op jit(solution)/shard_map/all_to_all | solution.py:61
  281.7 0.3 convert_reduce_fusion
  282.0 1.3 convolution_bitcast_fusion
  283.3 0.0 reduce-scatter.2.cloned.1.call-update
  283.3 38.7 %reduce-scatter.2.cloned.1.call-done = f32[8,1792]{1,0:T(8,128)} async-done(((f32[64,1792]{1,0:T(8,128)}), f32[8,1792]{1,0:T(8,128)}) %reduce-scatter.2.cloned.1.call-update) | async-done | bytes 57360 | tf_op jit(solution)/shard_map/reduce_scatter | solution.py:73
  321.9 1.4 convert_bitcast_fusion
  (7 shorter events, 0.1 us)
Async XLA Ops:
  6.5 170.1 %copy-start = (bf16[1,1792,256]{2,1,0:T(8,128)(2,1)S(1)}, bf16[1,1792,256]{2,1,0:T(8,128)(2,1)}, u32[]{:S(2)}) copy-start(bf16[1,1792,256]{2,1,0:T(8,128)(2,1)} %param.13) | copy-start | bytes 2752516
  6.5 170.1 %all-reduce.2.cloned.1.call-start = ((), (), s32[]{:S(2)}) async-start(), calls=%async_computation.4 | async-start | bytes 1048576 | tf_op jit(solution)/shard_map/psum | solution.py:45
  34.5 100.4 %copy-start.6 = (bf16[1,256,1792]{2,1,0:T(8,128)(2,1)S(1)}, bf16[1,256,1792]{2,1,0:T(8,128)(2,1)}, u32[]{:S(2)}) copy-start(bf16[1,256,1792]{2,1,0:T(8,128)(2,1)} %param.15) | copy-start | bytes 2752516
  135.0 1.6 copy-start.5
  135.0 41.6 %copy-start.2 = (bf16[1,64,8,256]{3,2,1,0:T(8,128)(2,1)S(1)}, bf16[1,64,8,256]{3,2,1,0:T(8,128)(2,1)}, u32[]{:S(2)}) copy-start(bf16[1,64,8,256]{3,2,1,0:T(8,128)(2,1)} %param.11) | copy-start | bytes 786436
  135.0 41.6 %copy-start.4 = (bf16[1,64,8,256]{3,2,1,0:T(8,128)(2,1)S(1)}, bf16[1,64,8,256]{3,2,1,0:T(8,128)(2,1)}, u32[]{:S(2)}) copy-start(bf16[1,64,8,256]{3,2,1,0:T(8,128)(2,1)} %param.12) | copy-start | bytes 786436
  136.5 185.5 %reduce-scatter.2.cloned.1.call-start = ((), (), s32[]{:S(2)}) async-start(), calls=%async_computation.5 | async-start | bytes 516096 | tf_op jit(solution)/shard_map/reduce_scatter | solution.py:73
  159.6 19.0 %copy-start.3 = (bf16[1,1792,256]{2,1,0:T(8,128)(2,1)S(1)}, bf16[1,1792,256]{2,1,0:T(8,128)(2,1)}, u32[]{:S(2)}) copy-start(bf16[1,1792,256]{2,1,0:T(8,128)(2,1)} %param.14) | copy-start | bytes 2752516
  176.6 2.0 copy-start.1
Sparse Core Ops, SparseCore 0:
  136.6 39.9 all-reduce.1
  283.4 38.4 reduce-scatter.1
where the time goes:
time: 331 us; the launch traced here: 330 us
  blocking collectives  252 us (76%)
  waiting for transfers between devices  55.7 us (17%)
  between operations  13.5 us (4%)
  matrix products  5.72 us (2%)
    all_to_all x1, blocking collectives, per_device(): lax.all_to_all(part_grad, 'node', split_axis=0, concat_axis=0, tiled=True)  102 us
    all_to_all x1, blocking collectives, per_device(): lax.all_to_all(send_rows, 'node', split_axis=0, concat_axis=0, tiled=True)  100 us
    reduce_scatter x1, waiting for transfers between devices, per_device(): lax.psum_scatter(token_grad, 'group', scatter_dimension=0, tiled=True)  38.7 us
    all_gather x1, blocking collectives, per_device(): relay_rows = lax.all_gather(out_grad, 'group', axis=1, tiled=True)[0]  26.5 us
    all_to_all x1, blocking collectives, per_device(): lax.all_to_all(send_weight, 'node', split_axis=0, concat_axis=0, tiled=True)  22.7 us
    psum x1, waiting for transfers between devices, per_device(): hidden_grad = lax.psum(partial_hidden, 'tp')  17 us
  transfers between devices with their start and end apart: 2, of which 2 were waited for; matrix products, arithmetic and copies ran while one was open for 0% of the time, Pallas kernels for 0%

commit v1 on v0

v1 whole, which is shorter than its diff:
```python
import functools

import jax
import jax.numpy as jnp
from jax import lax
from jax.experimental import pallas as pl
from jax.experimental.pallas import tpu as pltpu
from jax.sharding import PartitionSpec as P

MESH = pl.DeviceIdType.MESH
NX, NZ, TEAM, TEAMS, Q = 4, 16, 4, 4, 8
FAR = 11
BF16, F32 = jnp.bfloat16, jnp.float32


def travels(i, s, d):
    if d == 0:
        return s <= 3 - i
    if d == 1:
        return s <= 7 - i
    return jnp.logical_and(s <= 11 - i, i >= 2)


def kernel(
    ny, og_ref, ids_ref, sc_ref, sg_hbm, su_hbm, wg_hbm, wu_hbm, wd_hbm, out_ref,
    sg, su, wg, wu, wd, relay, packed, rbuf, hsend, hrecv, pg, gbuf, fsum, ybuf, ysend, yrecv,
    load_sem, y_send, y_recv, x_send, x_recv, z_send, z_recv, h_send, h_recv,
    b_send, b_recv, c_send, c_recv, o_send, o_recv,
):
    y = lax.axis_index("group")
    node = lax.axis_index("node")
    c = lax.axis_index("tp")
    x, z = node // NZ, lax.rem(node, NZ)
    team, j = z // TEAM, lax.rem(z, TEAM)
    feat = og_ref.shape[1]
    rows = ny * Q

    def at_y(k):
        return {"group": lax.rem(y + k, ny)}

    def at_x(k):
        return {"node": lax.rem(x + k, NX) * NZ + z}

    def at_z(k):
        return {"node": x * NZ + lax.rem(z + k + NZ, NZ)}

    other = {"tp": 1 - c}
    loads = [
        pltpu.make_async_copy(src, dst, load_sem.at[n])
        for n, (src, dst) in enumerate(((sg_hbm, sg), (su_hbm, su), (wd_hbm, wd), (wg_hbm, wg), (wu_hbm, wu)))
    ]
    for load in loads:
        load.start()

    barrier = pltpu.get_barrier_semaphore()
    partners = [at_y(k) for k in range(1, ny)] + [at_x(k) for k in range(1, NX)] + [at_z(1), at_z(-1), other]
    for partner in partners:
        pl.semaphore_signal(barrier, inc=1, device_id=partner, device_id_type=MESH)
    pl.semaphore_wait(barrier, len(partners))

    def remote(src, dst, send, recv, where):
        return pltpu.make_async_remote_copy(
            src_ref=src, dst_ref=dst, send_sem=send, recv_sem=recv, device_id=where, device_id_type=MESH
        )

    def y_copy(k):
        return remote(og_ref, relay.at[y], y_send.at[k], y_recv.at[k], at_y(k))

    for k in range(1, ny):
        y_copy(k).start()
    relay[pl.ds(y, 1)] = og_ref[...][None]

    lanes = NX * TEAMS * Q
    lane = lax.broadcasted_iota(jnp.int32, (rows, lanes), 1)
    expert = lane // Q + y * (NX * TEAMS)
    pick = jnp.zeros((rows, lanes), F32)
    weight = jnp.zeros((rows, lanes), F32)
    ids = ids_ref[...]
    scores = sc_ref[...].astype(F32)
    for k in range(ids.shape[1]):
        hit = ids[:, k : k + 1] == expert
        pick = jnp.where(hit, 1.0, pick)
        weight = jnp.where(hit, scores[:, k : k + 1], weight)
    before = lax.broadcasted_iota(jnp.int32, (rows, rows), 1) < lax.broadcasted_iota(jnp.int32, (rows, rows), 0)
    slot = jnp.dot(before.astype(BF16), pick.astype(BF16), preferred_element_type=F32)
    placed = jnp.logical_and(slot == lax.rem(lane, Q).astype(F32), pick > 0.5)
    place = jnp.where(placed, 1.0, 0.0).astype(BF16)
    place_weight = jnp.where(placed, weight, 0.0).astype(BF16)

    for k in range(1, ny):
        y_copy(k).wait_recv()
    pack = lax.dot_general(
        place, relay[...].reshape(rows, feat), (((0,), (0,)), ((), ())), preferred_element_type=F32
    ).astype(BF16)
    packed[...] = pack.reshape(NX, TEAMS, Q, feat)

    def x_copy(k):
        to = lax.rem(x + k, NX)
        return remote(packed.at[to], rbuf.at[z, :, x], x_send.at[k], x_recv.at[k], at_x(k))

    for k in (2, 1, 3):
        x_copy(k).start()
    rbuf[pl.ds(z, 1), :, pl.ds(x, 1)] = packed[pl.ds(x, 1)][:, :, None]
    for k in range(1, NX):
        x_copy(k).wait_recv()

    def place_of(way, distance):
        src = lax.rem(z - distance + NZ, NZ) if way == 0 else lax.rem(z + distance, NZ)
        at = lax.rem(src, TEAM)
        return src, src // TEAM, (at if way == 0 else TEAM - 1 - at)

    def z_copy(way, s, d):
        src, home, _ = place_of(way, s - 1)
        t = lax.rem(home + (d if way == 0 else TEAMS - d), TEAMS)
        piece = rbuf.at[src, t]
        return remote(piece, piece, z_send.at[way, s, d], z_recv.at[way, s, d], at_z(1 if way == 0 else -1))

    def z_arrive(way, s, d):
        src, home, _ = place_of(way, s)
        t = lax.rem(home + (d if way == 0 else TEAMS - d), TEAMS)
        piece = rbuf.at[src, t]
        return remote(piece, piece, z_send.at[way, s, d], z_recv.at[way, s, d], at_z(1 if way == 0 else -1))

    def z_step(s):
        for d in (2, 1, 0):
            for way in (0, 1):
                if s > 1:
                    _, _, i = place_of(way, s - 1)

                    @pl.when(travels(i, s - 1, d))
                    def _():
                        z_arrive(way, s - 1, d).wait_recv()

                if s <= FAR:
                    _, _, i = place_of(way, s - 1)

                    @pl.when(travels(i, s, d))
                    def _():
                        z_copy(way, s, d).start()

    def hidden_part(n, u):
        rows_in = rbuf[pl.ds(u * TEAM, TEAM), pl.ds(team, 1)].reshape(TEAM * NX * Q, feat)
        hsend[n] = lax.dot_general(rows_in, wd[...], (((1,), (1,)), ((), ())), preferred_element_type=F32)
        h_copy(n).start()

    def h_copy(n):
        return remote(hsend.at[n], hrecv.at[n], h_send.at[n], h_recv.at[n], other)

    def expert_part(n, u):
        h_copy(n).wait_recv()
        grad = hsend[n] + hrecv[n]

        def saved(ref):
            parts = [ref[k, pl.ds(u * TEAM, TEAM)][:, None] for k in range(NX)]
            return jnp.concatenate(parts, axis=1).reshape(TEAM * NX * Q, -1).astype(F32)

        g, up = saved(sg), saved(su)
        s = jax.nn.sigmoid(g)
        gate_grad = (grad * up * s * (1.0 + g * (1.0 - s))).astype(BF16)
        up_grad = (grad * g * s).astype(BF16)
        nt = (((1,), (1,)), ((), ()))
        part = lax.dot_general(gate_grad, wg[...], nt, preferred_element_type=F32)
        part = part + lax.dot_general(up_grad, wu[...], nt, preferred_element_type=F32)
        pg[pl.ds(u * TEAM, TEAM)] = part.astype(BF16).reshape(TEAM, NX, Q, feat)

    for s in range(1, 5):
        z_step(s)
    for load in loads:
        load.wait()
    hidden_part(0, team)
    z_step(5)
    expert_part(0, team)
    for s in range(6, 9):
        z_step(s)
    up_team, down_team = lax.rem(team + 1, TEAMS), lax.rem(team + 3, TEAMS)
    hidden_part(1, up_team)
    hidden_part(2, down_team)
    z_step(9)
    expert_part(1, up_team)
    expert_part(2, down_team)
    for s in range(10, FAR + 2):
        z_step(s)
    across = lax.rem(team + 2, TEAMS)
    hidden_part(3, across)
    expert_part(3, across)

    def b_copy(way, s, d, own_only):
        src, home, _ = place_of(way, s)
        t = lax.rem(home + (d if way == 0 else TEAMS - d), TEAMS)
        piece = gbuf.at[way, src, t]
        return remote(
            pg.at[src] if own_only else piece, piece, b_send.at[way, s, d], b_recv.at[way, s, d],
            at_z(-1 if way == 0 else 1),
        )

    def b_arrive(way, s, d):
        src, home, _ = place_of(way, s)
        t = lax.rem(home + (d if way == 0 else TEAMS - d), TEAMS)
        piece = gbuf.at[way, src, t]
        return remote(
            piece, piece, b_send.at[way, s + 1, d], b_recv.at[way, s + 1, d], at_z(-1 if way == 0 else 1)
        )

    for s in range(FAR, 0, -1):
        for d in (2, 1, 0):
            for way in (0, 1):
                src, home, i = place_of(way, s)
                t = lax.rem(home + (d if way == 0 else TEAMS - d), TEAMS)
                last = travels(i, s, d)
                if s < FAR:
                    further = travels(i, s + 1, d)

                    @pl.when(further)
                    def _():
                        b_arrive(way, s, d).wait_recv()

                        @pl.when(t == team)
                        def _():
                            mine = pg[pl.ds(src, 1)].astype(F32)
                            sofar = gbuf[way, pl.ds(src, 1), pl.ds(t, 1)][0].astype(F32)
                            gbuf[way, pl.ds(src, 1), pl.ds(t, 1)] = (mine + sofar).astype(BF16)[None]

                        b_copy(way, s, d, False).start()

                    last = jnp.logical_and(last, jnp.logical_not(further))

                @pl.when(last)
                def _():
                    b_copy(way, s, d, True).start()

    fsum[...] = jnp.zeros_like(fsum)
    fsum[pl.ds(team, 1)] = pg[pl.ds(z, 1)]
    for d in (0, 1, 2):
        for way in (0, 1):
            _, home, i = place_of(way, 0)
            t = lax.rem(home + (d if way == 0 else TEAMS - d), TEAMS)

            @pl.when(travels(i, 1, d))
            def _():
                b_arrive(way, 0, d).wait_recv()
                came = gbuf[way, pl.ds(z, 1), pl.ds(t, 1)][0].astype(F32)
                fsum[pl.ds(t, 1)] = (fsum[pl.ds(t, 1)].astype(F32) + came).astype(BF16)

    def c_copy(k):
        to = lax.rem(x + k, NX)
        return remote(fsum.at[:, to], ybuf.at[x], c_send.at[k], c_recv.at[k], at_x(k))

    for k in (2, 1, 3):
        c_copy(k).start()
    ybuf[pl.ds(x, 1)] = fsum[:, pl.ds(x, 1)].reshape(1, TEAMS, Q, feat)
    for k in range(1, NX):
        c_copy(k).wait_recv()
    token = jnp.dot(place_weight, ybuf[...].reshape(lanes, feat), preferred_element_type=F32)
    ysend[...] = token.astype(BF16).reshape(ny, Q, feat)

    def o_copy(k):
        return remote(ysend.at[lax.rem(y + k, ny)], yrecv.at[k], o_send.at[k], o_recv.at[k], at_y(k))

    for k in range(1, ny):
        o_copy(k).start()
    total = ysend[pl.ds(y, 1)][0].astype(F32)
    for k in range(1, ny):
        o_copy(k).wait_recv()
        total = total + yrecv[k].astype(F32)
    out_ref[...] = total.astype(BF16)

    for k in range(1, ny):
        y_copy(k).wait_send()
        o_copy(k).wait_send()
    for k in range(1, NX):
        x_copy(k).wait_send()
        c_copy(k).wait_send()
    for n in range(TEAMS):
        h_copy(n).wait_send()
    for s in range(1, FAR + 1):
        for d in (2, 1, 0):
            for way in (0, 1):
                _, _, i = place_of(way, s - 1)

                @pl.when(travels(i, s, d))
                def _():
                    z_copy(way, s, d).wait_send()

                _, _, i = place_of(way, s)

                @pl.when(travels(i, s, d))
                def _():
                    b_copy(way, s, d, False).wait_send()


def per_device(ny, out_grad, expert_ids, gate_scores, saved_gate, saved_up, w_gate, w_up, w_down):
    feat = out_grad.shape[2]
    hid = w_down.shape[1]
    vmem = pl.BlockSpec(memory_space=pltpu.VMEM)
    hbm = pl.BlockSpec(memory_space=pl.ANY)
    saved_shape = (NX, NZ, Q, hid)
    dma = pltpu.SemaphoreType.DMA
    out = pl.pallas_call(
        functools.partial(kernel, ny),
        out_shape=jax.ShapeDtypeStruct((Q, feat), BF16),
        in_specs=[vmem] * 3 + [hbm] * 5,
        out_specs=vmem,
        scratch_shapes=[
            pltpu.VMEM(saved_shape, BF16),
            pltpu.VMEM(saved_shape, BF16),
            pltpu.VMEM((feat, hid), BF16),
            pltpu.VMEM((feat, hid), BF16),
            pltpu.VMEM((hid, feat), BF16),
            pltpu.VMEM((ny, Q, feat), BF16),
            pltpu.VMEM((NX, TEAMS, Q, feat), BF16),
            pltpu.VMEM((NZ, TEAMS, NX, Q, feat), BF16),
            pltpu.VMEM((TEAMS, TEAM * NX * Q, hid), F32),
            pltpu.VMEM((TEAMS, TEAM * NX * Q, hid), F32),
            pltpu.VMEM((NZ, NX, Q, feat), BF16),
            pltpu.VMEM((2, NZ, TEAMS, NX, Q, feat), BF16),
            pltpu.VMEM((TEAMS, NX, Q, feat), BF16),
            pltpu.VMEM((NX, TEAMS, Q, feat), BF16),
            pltpu.VMEM((ny, Q, feat), BF16),
            pltpu.VMEM((ny, Q, feat), BF16),
            dma((5,)),
            dma((ny,)),
            dma((ny,)),
            dma((NX,)),
            dma((NX,)),
            dma((2, FAR + 1, 3)),
            dma((2, FAR + 1, 3)),
            dma((TEAMS,)),
            dma((TEAMS,)),
            dma((2, FAR + 1, 3)),
            dma((2, FAR + 1, 3)),
            dma((NX,)),
            dma((NX,)),
            dma((ny,)),
            dma((ny,)),
        ],
        compiler_params=pltpu.CompilerParams(
            collective_id=0, has_side_effects=True, vmem_limit_bytes=56 * 1024 * 1024
        ),
        name="routed_backward",
    )(
        out_grad[0],
        expert_ids[0],
        gate_scores[0],
        saved_gate.reshape(saved_shape),
        saved_up.reshape(saved_shape),
        w_gate[0],
        w_up[0],
        w_down[0],
    )
    return out[None]


def solution(mesh):
    placed = (
        P("node", "group", "tp"),
        P("node", None, None),
        P("node", None, None),
        P(("group", "node"), None, None, None),
        P(("group", "node"), None, None, None),
        P(("group", "node"), "tp", None),
        P(("group", "node"), "tp", None),
        P(("group", "node"), None, "tp"),
    )
    return jax.shard_map(
        functools.partial(per_device, mesh.shape["group"]),
        mesh=mesh,
        in_specs=placed,
        out_specs=P("node", "group", "tp"),
        check_vma=False,
    )
```

time: 331 us -> 147 us (0.44)
  the two profiles are of different devices: /device:TPU:6 before, /device:TPU:64 now
where the time goes in v1:
time: 147 us; the launch traced here: 146 us
  Pallas kernels  143 us (97%)
  local copies, waits for them, and re-layouts  3.43 us (2%)
    pallas_call x1, Pallas kernels, per_device(): pl.pallas_call(functools.partial(kernel, ny), out_shape=jax.ShapeDtypeStr...  143 us
    unnamed x7, local copies, waits for them, and re-layouts  3.43 us

profile of v1, /device:TPU:64, one launch (start us, length us, event | category | flops | bytes accessed | tf_op | source)
XLA Modules:
  0.0 146.3 jit_solution(11660802634954227345)
XLA Ops:
  0.0 0.0 copy-start.1
  0.0 0.7 copy-done.1
  0.7 0.0 copy-start
  0.7 0.7 copy.10
  1.4 0.0 copy-done
  1.4 0.7 copy.9
  2.1 142.8 %routed_backward.1 = bf16[8,1792]{1,0:T(8,128)(2,1)} custom-call(bf16[8,1792]{1,0:T(8,128)(2,1)} %bitcast.17, s32[64,8]{1,0:T(8,128)} %bitcast.14, bf16[64,8]{1,0:T(8,128)(2,1)} %bitcast.16, bf16[4,16,8,256]{3,2,1,0:T(8,128)(2,1)} %bitcast.12, bf16[4,16,8,256]{3,2,1,0:T(8,128)(2,1)} %bitcast.13, bf16[1792,256]{1,0:T(8,128)(2,1)} %bitcast.9, ...), custom_call_target="tpu_custom_call" | custom-call | tf_op jit(solution)/shard_map/routed_backward/pallas_call | solution.py:298
  144.9 1.4 copy.12
Async XLA Ops:
  0.0 0.7 copy-start.1
  0.7 0.7 copy-start

commit v2 on v1

v2 whole, which is shorter than its diff:
```python
import functools

import jax
import jax.numpy as jnp
from jax import lax
from jax.experimental import pallas as pl
from jax.experimental.pallas import tpu as pltpu
from jax.sharding import PartitionSpec as P

MESH = pl.DeviceIdType.MESH
NX, NZ, TEAM, TEAMS, Q = 4, 16, 4, 4, 8
FAR = 5
RAW = (8, 7)
PAIRS, OWN = 4, 4
META = 128
BF16, F32 = jnp.bfloat16, jnp.float32
NT = (((1,), (1,)), ((), ()))
TN = (((0,), (0,)), ((), ()))


def travels(i, s, d):
    return s <= (3 - i if d == 0 else 5 - i)


def y_steps(p):
    return (4, 3) if p % 2 == 0 else (3, 4)


def kernel(
    ny, og_ref, ids_ref, sc_ref, sg_hbm, su_hbm, wg_hbm, wu_hbm, wd_hbm, out_ref,
    sg, su, wg, wu, wd, msg, raw, yown, ypair, pw_own, pw_pair, packed, xpack, rbuf, zbuf, hsend, hrecv,
    pg, pgz, gbuf, fsum, ybuf, cbuf, tok, tok_own, ysr, yso, rs, zret,
    load_sem, raw_send, raw_recv, y_send, y_recv, xo_send, xo_recv, xz_send, xz_recv, z_send, z_recv,
    h_send, h_recv, b_send, b_recv, co_send, co_recv, cz_send, cz_recv, r_send, r_recv, v_send, v_recv,
):
    y = lax.axis_index("group")
    node = lax.axis_index("node")
    c = lax.axis_index("tp")
    x, z = node // NZ, lax.rem(node, NZ)
    team, j = z // TEAM, lax.rem(z, TEAM)
    feat = og_ref.shape[1]
    rows = ny * Q

    def at_y(k):
        return {"group": lax.rem(y + k + ny, ny)}

    def at_x(k):
        return {"node": lax.rem(x + k, NX) * NZ + z}

    def at_z(k):
        return {"node": x * NZ + lax.rem(z + k + NZ, NZ)}

    other = {"tp": 1 - c}
    loads = [
        pltpu.make_async_copy(src, dst, load_sem.at[n])
        for n, (src, dst) in enumerate(((sg_hbm, sg), (su_hbm, su), (wd_hbm, wd), (wg_hbm, wg), (wu_hbm, wu)))
    ]
    for load in loads:
        load.start()

    barrier = pltpu.get_barrier_semaphore()
    partners = [at_y(1), at_y(-1)] + [at_x(k) for k in range(1, NX)] + [other]
    partners += [at_z(way * k) for k in (1, 3, 4, 5, 6) for way in (1, -1)]
    for partner in partners:
        pl.semaphore_signal(barrier, inc=1, device_id=partner, device_id_type=MESH)

    one = lax.broadcasted_iota(jnp.int32, (rows, rows), 0) == lax.broadcasted_iota(jnp.int32, (rows, rows), 1)
    one = one.astype(BF16)
    ids_t = lax.dot_general(ids_ref[...].astype(F32).astype(BF16), one, TN, preferred_element_type=F32)
    sc_t = lax.dot_general(sc_ref[...], one, TN, preferred_element_type=F32)
    msg[:, :feat] = og_ref[...]
    msg[:, feat:] = jnp.concatenate([ids_t, sc_t], axis=1).astype(BF16)
    yown[pl.ds(y, 1)] = og_ref[...][None]
    pl.semaphore_wait(barrier, len(partners))

    def remote(src, dst, send, recv, where):
        return pltpu.make_async_remote_copy(
            src_ref=src, dst_ref=dst, send_sem=send, recv_sem=recv, device_id=where, device_id_type=MESH
        )

    def raw_first(way):
        k = 6 - j if way == 0 else j + 3
        return remote(
            msg, raw.at[way, k], raw_send.at[way, 0], raw_recv.at[way, k], at_z(k if way == 0 else -k)
        )

    def raw_copy(way, s):
        return remote(
            raw.at[way, s - 1], raw.at[way, s], raw_send.at[way, s], raw_recv.at[way, s], at_z(1 - 2 * way)
        )

    def takes(way, s):
        if s == 3:
            return j == 2 - way, 0
        if s == 4:
            return (j >= 2, 3 - j) if way == 0 else (j <= 1, j)
        if s == 5:
            return (j != 1, (j == 2).astype(jnp.int32) + 1) if way == 0 else (j != 2, 2)
        return True, {(0, 6): 3, (1, 6): 4, (0, 7): 5, (1, 7): 6, (0, 8): 7}[way, s]

    def source(m):
        if m == 0:
            off = jnp.where(j == 0, 4, jnp.where(j == 1, 3, jnp.where(j == 2, -3, -4)))
        elif m == 1:
            off = jnp.where(j == 0, -5, jnp.where(j == 1, 4, jnp.where(j == 2, -4, -5)))
        elif m == 2:
            off = jnp.where(j == 2, -5, 5)
        else:
            off = {3: -6, 4: 6, 5: -7, 6: 7, 7: -8}[m]
        return lax.rem(z + off + NZ, NZ)

    def when(condition):
        if condition is True:
            return lambda body: body()
        return pl.when(condition)

    def raw_step(s):
        for way in (0, 1):
            if s > RAW[way]:
                continue
            condition, m = takes(way, s)

            @when(condition)
            def _():
                raw_copy(way, s).wait_recv()
                if s < RAW[way]:
                    raw_copy(way, s + 1).start()
                block = raw[way, s]
                p, h = m // 2, m % 2
                ypair[pl.ds(p, 1), pl.ds(y, 1), pl.ds(h, 1)] = block[:, :feat][None, None, None]
                place_in(block[:, feat:].astype(F32), m)

    def y_buf(p):
        return yown if p == OWN else ypair.at[p]

    def y_copy(p, way, s):
        piece = y_buf(p).at[lax.rem(y + (1 - s if way == 0 else s - 1) + ny, ny)]
        return remote(piece, piece, y_send.at[p, way, s], y_recv.at[p, way, s], at_y(1 - 2 * way))

    def y_arrive(p, way, s):
        piece = y_buf(p).at[lax.rem(y + (-s if way == 0 else s) + ny, ny)]
        return remote(piece, piece, y_send.at[p, way, s], y_recv.at[p, way, s], at_y(1 - 2 * way))

    def y_step(p, s):
        for way in (0, 1):
            steps = y_steps(p)[way]
            if 2 <= s <= steps + 1:
                y_arrive(p, way, s - 1).wait_recv()
            if s <= steps:
                y_copy(p, way, s).start()

    def placing(meta, expert, place_in_expert):
        shape = expert.shape
        pick = jnp.zeros(shape, F32)
        weight = jnp.zeros(shape, F32)
        for k in range(Q):
            hit = meta[k : k + 1, :rows] == expert
            pick = jnp.where(hit, 1.0, pick)
            weight = jnp.where(hit, meta[k : k + 1, rows:], weight)
        before = lax.broadcasted_iota(jnp.int32, (rows, rows), 0) < lax.broadcasted_iota(jnp.int32, (rows, rows), 1)
        slot = jnp.dot(pick.astype(BF16), before.astype(F32).astype(BF16), preferred_element_type=F32)
        placed = jnp.logical_and(slot == place_in_expert, pick > 0.5)
        return jnp.where(placed, 1.0, 0.0).astype(BF16), jnp.where(placed, weight, 0.0).astype(BF16)

    def place_in(meta, m):
        line = lax.broadcasted_iota(jnp.int32, (NX * Q, rows), 0)
        expert = (line // Q * TEAMS + (y * (NX * TEAMS) + team)).astype(F32)
        place, weighted = placing(meta, expert, lax.rem(line, Q).astype(F32))
        pw_pair[pl.ds(m, 1), pl.ds(0, 1)] = place[None, None]
        pw_pair[pl.ds(m, 1), pl.ds(1, 1)] = weighted[None, None]

    def xz_copy(p, k):
        to = lax.rem(x + k, NX)
        return remote(xpack.at[p, to], zbuf.at[p, x], xz_send.at[p, k], xz_recv.at[p, k], at_x(k))

    def pack_pair(p):
        y_step(p, 5)
        for h in (0, 1):
            packs = jnp.dot(
                pw_pair[2 * p + h, 0], ypair[p, :, h].reshape(rows, feat), preferred_element_type=F32
            ).astype(BF16)
            xpack[p, :, h] = packs.reshape(NX, Q, feat)
        for k in (2, 1, 3):
            xz_copy(p, k).start()
        zbuf[p, pl.ds(x, 1)] = xpack[p, pl.ds(x, 1)]

    def near(d):
        return lax.rem(team + d + TEAMS, TEAMS)

    def xo_copy(d, k):
        to = lax.rem(x + k, NX)
        t = near(d)
        return remote(
            packed.at[t, to], rbuf.at[z, t, x], xo_send.at[d + 1, k], xo_recv.at[d + 1, k], at_x(k)
        )

    def pack_own():
        y_step(OWN, 5)
        line = lax.broadcasted_iota(jnp.int32, (TEAMS * NX * Q, rows), 0)
        expert = lax.rem(line // Q, NX) * TEAMS + line // (NX * Q) + y * (NX * TEAMS)
        place, weighted = placing(msg[:, feat:].astype(F32), expert.astype(F32), lax.rem(line, Q).astype(F32))
        pw_own[...] = weighted
        packs = jnp.dot(place, yown[...].reshape(rows, feat), preferred_element_type=F32).astype(BF16)
        packed[...] = packs.reshape(TEAMS, NX, Q, feat)
        for d in (1, -1, 0):
            for k in (2, 1, 3):
                xo_copy(d, k).start()
        rbuf[pl.ds(z, 1), :, pl.ds(x, 1)] = packed[:, pl.ds(x, 1)][None]

    def place_of(way, distance):
        src = lax.rem(z - distance + NZ, NZ) if way == 0 else lax.rem(z + distance, NZ)
        at = lax.rem(src, TEAM)
        return src, src // TEAM, (at if way == 0 else TEAM - 1 - at)

    def piece_of(way, distance, d):
        src, home, _ = place_of(way, distance)
        return src, lax.rem(home + (d if way == 0 else TEAMS - d), TEAMS)

    def z_copy(way, s, d, distance):
        src, t = piece_of(way, distance, d)
        piece = rbuf.at[src, t]
        return remote(piece, piece, z_send.at[way, s, d], z_recv.at[way, s, d], at_z(1 - 2 * way))

    def z_step(s):
        for d in (1, 0):
            for way in (0, 1):
                _, _, i = place_of(way, s - 1)
                if s > 1:

                    @pl.when(travels(i, s - 1, d))
                    def _():
                        z_copy(way, s - 1, d, s - 1).wait_recv()

                if s <= FAR:

                    @pl.when(travels(i, s, d))
                    def _():
                        z_copy(way, s, d, s - 1).start()

    def h_copy(n):
        return remote(hsend.at[n], hrecv.at[n], h_send.at[n], h_recv.at[n], other)

    def hidden_part(n, rows_in):
        hsend[n] = lax.dot_general(rows_in.reshape(-1, feat), wd[...], NT, preferred_element_type=F32)
        h_copy(n).start()

    def expert_part(n, saved):
        h_copy(n).wait_recv()
        grad = hsend[n] + hrecv[n]
        g, up = saved(sg), saved(su)
        s = jax.nn.sigmoid(g)
        gate_grad = (grad * up * s * (1.0 + g * (1.0 - s))).astype(BF16)
        up_grad = (grad * g * s).astype(BF16)
        part = lax.dot_general(gate_grad, wg[...], NT, preferred_element_type=F32)
        part = part + lax.dot_general(up_grad, wu[...], NT, preferred_element_type=F32)
        return part.astype(BF16)

    def team_hidden(n, u):
        hidden_part(n, rbuf[pl.ds(u * TEAM, TEAM), pl.ds(team, 1)])

    def team_expert(n, u):
        def saved(ref):
            parts = [ref[k, pl.ds(u * TEAM, TEAM)][:, None] for k in range(NX)]
            return jnp.concatenate(parts, axis=1).reshape(TEAM * NX * Q, -1).astype(F32)

        pg[pl.ds(u * TEAM, TEAM)] = expert_part(n, saved).reshape(TEAM, NX, Q, feat)

    def pairs_hidden(n, first):
        for p in (first, first + 1):
            for k in range(1, NX):
                xz_copy(p, k).wait_recv()
        hidden_part(n, zbuf[pl.ds(first, 2)])

    def pairs_expert(n, first):
        def saved(ref):
            parts = [
                ref[k, pl.ds(source(2 * p + h), 1)]
                for p in (first, first + 1)
                for k in range(NX)
                for h in (0, 1)
            ]
            return jnp.concatenate(parts, axis=0).reshape(2 * NX * 2 * Q, -1).astype(F32)

        pgz[pl.ds(first, 2)] = expert_part(n, saved).reshape(2, NX, 2, Q, feat)
        for p in (first + 1, first):
            for k in (2, 1, 3):
                cz_copy(p, k).start()
            cbuf[p, pl.ds(x, 1)] = pgz[p, pl.ds(x, 1)]

    def b_copy(way, s, d, own_only):
        src, t = piece_of(way, s, d)
        piece = gbuf.at[way, src, t]
        return remote(
            pg.at[src] if own_only else piece, piece, b_send.at[way, s, d], b_recv.at[way, s, d],
            at_z(2 * way - 1),
        )

    def b_arrive(way, s, d):
        src, t = piece_of(way, s, d)
        piece = gbuf.at[way, src, t]
        return remote(piece, piece, b_send.at[way, s + 1, d], b_recv.at[way, s + 1, d], at_z(2 * way - 1))

    def b_step(s):
        for d in (1, 0):
            for way in (0, 1):
                _, _, i = place_of(way, s)
                src, t = piece_of(way, s, d)
                last = travels(i, s, d)
                if s < FAR:
                    further = travels(i, s + 1, d)

                    @pl.when(further)
                    def _():
                        b_arrive(way, s, d).wait_recv()

                        @pl.when(t == team)
                        def _():
                            mine = pg[pl.ds(src, 1)].astype(F32)
                            sofar = gbuf[way, pl.ds(src, 1), pl.ds(t, 1)][0].astype(F32)
                            gbuf[way, pl.ds(src, 1), pl.ds(t, 1)] = (mine + sofar).astype(BF16)[None]

                        b_copy(way, s, d, False).start()

                    last = jnp.logical_and(last, jnp.logical_not(further))

                @pl.when(last)
                def _():
                    b_copy(way, s, d, True).start()

    def came(way, d):
        b_arrive(way, 0, d).wait_recv()
        _, t = piece_of(way, 0, d)
        return gbuf[way, pl.ds(z, 1), pl.ds(t, 1)][0]

    def co_copy(d, k):
        to = lax.rem(x + k, NX)
        t = near(d)
        return remote(fsum.at[t, to], ybuf.at[t, x], co_send.at[d + 1, k], co_recv.at[d + 1, k], at_x(k))

    def cz_copy(p, k):
        to = lax.rem(x + k, NX)
        return remote(pgz.at[p, to], cbuf.at[p, x], cz_send.at[p, k], cz_recv.at[p, k], at_x(k))

    def to_relay(d):
        for k in (2, 1, 3):
            co_copy(d, k).start()
        t = near(d)
        ybuf[pl.ds(t, 1), pl.ds(x, 1)] = fsum[pl.ds(t, 1), pl.ds(x, 1)]

    def finish_tree():
        for way, d in ((0, 1), (1, -1)):
            fsum[pl.ds(near(d), 1)] = came(way, 1)
            to_relay(d)
        fsum[pl.ds(team, 1)] = pg[pl.ds(z, 1)]
        for way in (0, 1):
            _, _, i = place_of(way, 0)

            @pl.when(travels(i, 1, 0))
            def _():
                got = came(way, 0).astype(F32)
                fsum[pl.ds(team, 1)] = (fsum[pl.ds(team, 1)].astype(F32) + got).astype(BF16)

        to_relay(0)

    def combine_pair(p):
        for k in range(1, NX):
            cz_copy(p, k).wait_recv()
        for h in (0, 1):
            token = lax.dot_general(
                pw_pair[2 * p + h, 1], cbuf[p, :, h].reshape(NX * Q, feat), TN, preferred_element_type=F32
            )
            tok[p, :, h] = token.astype(BF16).reshape(ny, Q, feat)

    def combine_own():
        ybuf[pl.ds(near(2), 1)] = jnp.zeros((1, NX, Q, feat), BF16)
        for d in (1, -1, 0):
            for k in range(1, NX):
                co_copy(d, k).wait_recv()
        token = lax.dot_general(pw_own[...], ybuf[...].reshape(-1, feat), TN, preferred_element_type=F32)
        tok_own[...] = token.astype(BF16).reshape(ny, Q, feat)

    def r_bufs(p):
        return (tok_own, yso) if p == OWN else (tok.at[p], ysr.at[p])

    def r_target(p, way, s):
        left = y_steps(p)[way] + 1 - s
        return lax.rem(y + (left if way == 0 else -left) + ny, ny)

    def r_copy(p, way, s):
        mine, sums = r_bufs(p)
        src = mine.at[r_target(p, way, s)] if s == 1 else sums.at[way, s - 1]
        return remote(src, sums.at[way, s], r_send.at[p, way, s], r_recv.at[p, way, s], at_y(1 - 2 * way))

    def r_step(p, s):
        mine, sums = r_bufs(p)
        for way in (0, 1):
            steps = y_steps(p)[way]
            if 2 <= s <= steps + 1:
                r_copy(p, way, s - 1).wait_recv()
            if s <= steps:
                if s > 1:
                    term = mine[pl.ds(r_target(p, way, s), 1)][0].astype(F32)
                    sums[way, s - 1] = (sums[way, s - 1].astype(F32) + term).astype(BF16)
                r_copy(p, way, s).start()

    def r_total(p):
        r_step(p, 5)
        mine, sums = r_bufs(p)
        total = mine[pl.ds(y, 1)][0].astype(F32)
        for way in (0, 1):
            total = total + sums[way, y_steps(p)[way]].astype(F32)
        return total

    def r_finish(p):
        rs[pl.ds(2 * p, 2)] = r_total(p)

    def v_copy(way, s, first):
        to, where = (0, s) if first else (s - 1, 1)
        return remote(
            zret.at[way, s], zret.at[way, to], v_send.at[way, s], v_recv.at[way, to],
            at_z(-where if way == 0 else where),
        )

    def v_cases(way, s):
        condition, _ = takes(way, s)
        if s > 6:
            return ((True, False),)
        end = j == 2 - way
        if s == 3:
            return ((condition, True),)
        rest = jnp.logical_not(end)
        if condition is True:
            return ((end, True), (rest, False))
        return ((jnp.logical_and(condition, end), True), (jnp.logical_and(condition, rest), False))

    def v_step(s, way):
        condition, m = takes(way, s)

        @when(condition)
        def _():
            total = rs[pl.ds(m, 1)][0]
            if s < RAW[way]:
                v_copy(way, s + 1, False).wait_recv()
                total = total + zret[way, s].astype(F32)
            zret[way, s] = total.astype(BF16)

        for condition, first in v_cases(way, s):

            @when(condition)
            def _():
                v_copy(way, s, first).start()

    y_step(OWN, 1)
    raw_first(0).start()
    raw_first(1).start()
    raw_step(3)
    y_step(OWN, 2)
    raw_step(4)
    y_step(OWN, 3)
    raw_step(5)
    y_step(0, 1)
    y_step(OWN, 4)
    raw_step(6)
    y_step(1, 1)
    y_step(0, 2)
    pack_own()
    raw_step(7)
    y_step(2, 1)
    y_step(1, 2)
    y_step(0, 3)
    for d in (1, -1, 0):
        for k in range(1, NX):
            xo_copy(d, k).wait_recv()
    z_step(1)
    raw_step(8)
    y_step(3, 1)
    y_step(2, 2)
    y_step(1, 3)
    y_step(0, 4)
    z_step(2)
    y_step(3, 2)
    y_step(2, 3)
    y_step(1, 4)
    pack_pair(0)
    z_step(3)
    y_step(3, 3)
    y_step(2, 4)
    pack_pair(1)
    z_step(4)
    y_step(3, 4)
    pack_pair(2)
    for load in loads:
        load.wait()
    team_hidden(0, team)
    z_step(5)
    pack_pair(3)
    team_expert(0, team)
    z_step(6)
    beside = lax.rem(team + 3 - 2 * (j // 2), TEAMS)
    team_hidden(1, beside)
    pairs_hidden(2, 0)
    team_expert(1, beside)
    b_step(5)
    pairs_hidden(3, 2)
    pairs_expert(2, 0)
    b_step(4)
    pairs_expert(3, 2)
    b_step(3)
    combine_pair(3)
    r_step(3, 1)
    combine_pair(2)
    r_step(2, 1)
    r_step(3, 2)
    b_step(2)
    combine_pair(1)
    r_step(1, 1)
    r_step(2, 2)
    r_step(3, 3)
    combine_pair(0)
    r_step(0, 1)
    r_step(1, 2)
    r_step(2, 3)
    r_step(3, 4)
    b_step(1)
    r_finish(3)
    v_step(8, 0)
    v_step(7, 1)
    r_step(0, 2)
    r_step(1, 3)
    r_step(2, 4)
    finish_tree()
    r_finish(2)
    v_step(7, 0)
    v_step(6, 1)
    r_step(0, 3)
    r_step(1, 4)
    combine_own()
    r_step(OWN, 1)
    r_finish(1)
    v_step(6, 0)
    r_step(0, 4)
    r_step(OWN, 2)
    r_finish(0)
    for s in (5, 4, 3):
        for way in (0, 1):
            v_step(s, way)
        if s > 3:
            r_step(OWN, 8 - s)
    total = r_total(OWN)
    for way in (0, 1):
        v_copy(way, 1, False).wait_recv()
        total = total + zret[way, 0].astype(F32)
    out_ref[...] = total.astype(BF16)

    for way in (0, 1):
        raw_first(way).wait_send()
        for s in range(3, RAW[way] + 1):
            condition, _ = takes(way, s)
            if s < RAW[way]:

                @when(condition)
                def _():
                    raw_copy(way, s + 1).wait_send()

            @when(condition)
            def _():
                v_copy(way, s, False).wait_send()

        for p in range(PAIRS + 1):
            for s in range(1, y_steps(p)[way] + 1):
                y_copy(p, way, s).wait_send()
                r_copy(p, way, s).wait_send()
    for k in range(1, NX):
        for d in (1, -1, 0):
            xo_copy(d, k).wait_send()
            co_copy(d, k).wait_send()
        for p in range(PAIRS):
            xz_copy(p, k).wait_send()
            cz_copy(p, k).wait_send()
    for n in range(TEAMS):
        h_copy(n).wait_send()
    for s in range(1, FAR + 1):
        for d in (1, 0):
            for way in (0, 1):
                _, _, i = place_of(way, s - 1)

                @pl.when(travels(i, s, d))
                def _():
                    z_copy(way, s, d, s - 1).wait_send()

                _, _, i = place_of(way, s)

                @pl.when(travels(i, s, d))
                def _():
                    b_copy(way, s, d, False).wait_send()


def per_device(ny, out_grad, expert_ids, gate_scores, saved_gate, saved_up, w_gate, w_up, w_down):
    feat = out_grad.shape[2]
    hid = w_down.shape[1]
    vmem = pl.BlockSpec(memory_space=pltpu.VMEM)
    hbm = pl.BlockSpec(memory_space=pl.ANY)
    saved_shape = (NX, NZ, Q, hid)
    rows = ny * Q
    chunk = TEAM * NX * Q

    def sems(*shape):
        return [pltpu.SemaphoreType.DMA(shape)] * 2

    out = pl.pallas_call(
        functools.partial(kernel, ny),
        out_shape=jax.ShapeDtypeStruct((Q, feat), BF16),
        in_specs=[vmem] * 3 + [hbm] * 5,
        out_specs=vmem,
        scratch_shapes=[
            pltpu.VMEM(saved_shape, BF16),
            pltpu.VMEM(saved_shape, BF16),
            pltpu.VMEM((feat, hid), BF16),
            pltpu.VMEM((feat, hid), BF16),
            pltpu.VMEM((hid, feat), BF16),
            pltpu.VMEM((Q, feat + META), BF16),
            pltpu.VMEM((2, RAW[0] + 1, Q, feat + META), BF16),
            pltpu.VMEM((ny, Q, feat), BF16),
            pltpu.VMEM((PAIRS, ny, 2, Q, feat), BF16),
            pltpu.VMEM((TEAMS * NX * Q, rows), BF16),
            pltpu.VMEM((2 * PAIRS, 2, NX * Q, rows), BF16),
            pltpu.VMEM((TEAMS, NX, Q, feat), BF16),
            pltpu.VMEM((PAIRS, NX, 2, Q, feat), BF16),
            pltpu.VMEM((NZ, TEAMS, NX, Q, feat), BF16),
            pltpu.VMEM((PAIRS, NX, 2, Q, feat), BF16),
            pltpu.VMEM((4, chunk, hid), F32),
            pltpu.VMEM((4, chunk, hid), F32),
            pltpu.VMEM((NZ, NX, Q, feat), BF16),
            pltpu.VMEM((PAIRS, NX, 2, Q, feat), BF16),
            pltpu.VMEM((2, NZ, TEAMS, NX, Q, feat), BF16),
            pltpu.VMEM((TEAMS, NX, Q, feat), BF16),
            pltpu.VMEM((TEAMS, NX, Q, feat), BF16),
            pltpu.VMEM((PAIRS, NX, 2, Q, feat), BF16),
            pltpu.VMEM((PAIRS, ny, 2, Q, feat), BF16),
            pltpu.VMEM((ny, Q, feat), BF16),
            pltpu.VMEM((PAIRS, 2, 5, 2, Q, feat), BF16),
            pltpu.VMEM((2, 5, Q, feat), BF16),
            pltpu.VMEM((2 * PAIRS, Q, feat), F32),
            pltpu.VMEM((2, RAW[0] + 1, Q, feat), BF16),
            pltpu.SemaphoreType.DMA((5,)),
            *sems(2, RAW[0] + 1),
            *sems(PAIRS + 1, 2, 5),
            *sems(3, NX),
            *sems(PAIRS, NX),
            *sems(2, FAR + 1, 2),
            *sems(4),
            *sems(2, FAR + 1, 2),
            *sems(3, NX),
            *sems(PAIRS, NX),
            *sems(PAIRS + 1, 2, 5),
            *sems(2, RAW[0] + 1),
        ],
        compiler_params=pltpu.CompilerParams(
            collective_id=0, has_side_effects=True, vmem_limit_bytes=56 * 1024 * 1024
        ),
        name="routed_backward",
    )(
        out_grad[0],
        expert_ids[0],
        gate_scores[0],
        saved_gate.reshape(saved_shape),
        saved_up.reshape(saved_shape),
        w_gate[0],
        w_up[0],
        w_down[0],
    )
    return out[None]


def solution(mesh):
    placed = (
        P("node", "group", "tp"),
        P("node", None, None),
        P("node", None, None),
        P(("group", "node"), None, None, None),
        P(("group", "node"), None, None, None),
        P(("group", "node"), "tp", None),
        P(("group", "node"), "tp", None),
        P(("group", "node"), None, "tp"),
    )
    return jax.shard_map(
        functools.partial(per_device, mesh.shape["group"]),
        mesh=mesh,
        in_specs=placed,
        out_specs=P("node", "group", "tp"),
        check_vma=False,
    )
```

time: 147 us -> 130 us (0.88)
  the two profiles are of different devices: /device:TPU:64 before, /device:TPU:6 now
where the time goes in v2:
time: 130 us
  Pallas kernels  126 us (97%)
  local copies, waits for them, and re-layouts  3.43 us (3%)
    pallas_call x1, Pallas kernels, per_device(): pl.pallas_call(functools.partial(kernel, ny), out_shape=jax.ShapeDtypeStr...  126 us
    unnamed x7, local copies, waits for them, and re-layouts  3.43 us

profile of v2, /device:TPU:6, one launch (start us, length us, event | category | flops | bytes accessed | tf_op | source)
XLA Modules:
  0.0 129.7 jit_solution(12717166571906955172)
XLA Ops:
  0.0 0.0 copy-start.1
  0.0 0.7 copy-done.1
  0.7 0.0 copy-start
  0.7 0.7 copy.10
  1.4 0.0 copy-done
  1.4 0.7 copy.9
  2.1 126.2 %routed_backward.1 = bf16[8,1792]{1,0:T(8,128)(2,1)} custom-call(bf16[8,1792]{1,0:T(8,128)(2,1)} %bitcast.17, s32[64,8]{1,0:T(8,128)} %bitcast.14, bf16[64,8]{1,0:T(8,128)(2,1)} %bitcast.16, bf16[4,16,8,256]{3,2,1,0:T(8,128)(2,1)} %bitcast.12, bf16[4,16,8,256]{3,2,1,0:T(8,128)(2,1)} %bitcast.13, bf16[1792,256]{1,0:T(8,128)(2,1)} %bitcast.9, ...), custom_call_target="tpu_custom_call" | custom-call | tf_op jit(solution)/shard_map/routed_backward/pallas_call | solution.py:610
  128.3 1.4 %copy.12 = bf16[1,8,1792]{2,1,0:T(8,128)(2,1)} copy(bf16[1,8,1792]{2,1,0:T(8,128)(2,1)} %bitcast.15) | data formatting | bytes 57344
Async XLA Ops:
  0.0 0.7 copy-start.1
  0.7 0.7 copy-start

commit v3 on v2

--- a/solution.py
+++ b/solution.py
@@ -10,8 +10,7 @@
 MESH = pl.DeviceIdType.MESH
 NX, NZ, TEAM, TEAMS, Q = 4, 16, 4, 4, 8
 FAR = 5
-RAW = (8, 7)
-PAIRS, OWN = 4, 4
+PAIRS = 4
 META = 128
 BF16, F32 = jnp.bfloat16, jnp.float32
 NT = (((1,), (1,)), ((), ()))
@@ -29,9 +28,10 @@
 def kernel(
     ny, og_ref, ids_ref, sc_ref, sg_hbm, su_hbm, wg_hbm, wu_hbm, wd_hbm, out_ref,
     sg, su, wg, wu, wd, msg, raw, yown, ypair, pw_own, pw_pair, packed, xpack, rbuf, zbuf, hsend, hrecv,
-    pg, pgz, gbuf, fsum, ybuf, cbuf, tok, tok_own, ysr, yso, rs, zret,
-    load_sem, raw_send, raw_recv, y_send, y_recv, xo_send, xo_recv, xz_send, xz_recv, z_send, z_recv,
-    h_send, h_recv, b_send, b_recv, co_send, co_recv, cz_send, cz_recv, r_send, r_recv, v_send, v_recv,
+    pg, pgz, gbuf, fsum, ybuf, cbuf, tok, tok_own, ysr, ylast, rs, vmid, vfin,
+    load_sem, raw_send, raw_recv, own_send, own_recv, y_send, y_recv, xo_send, xo_recv, xz_send, xz_recv, z_send, z_recv,
+    h_send, h_recv, b_send, b_recv, co_send, co_recv, cz_send, cz_recv, r_send, r_recv, last_send, last_recv,
+    v_send, v_recv, f_send, f_recv,
 ):
     y = lax.axis_index("group")
     node = lax.axis_index("node")
@@ -59,17 +59,16 @@
         load.start()
 
     barrier = pltpu.get_barrier_semaphore()
-    partners = [at_y(1), at_y(-1)] + [at_x(k) for k in range(1, NX)] + [other]
-    partners += [at_z(way * k) for k in (1, 3, 4, 5, 6) for way in (1, -1)]
+    base = (5 + j - 4 * (j // 2), 8 - j - 4 * ((3 - j) // 2))
+    relays = (j + 1) % 2
+    partners = [at_y(k) for k in range(1, ny)] + [at_x(k) for k in range(1, NX)] + [other, at_z(1), at_z(-1)]
+    partners += [at_z(6 - j), at_z(8 - j), at_z(-3 - j), at_z(-5 - j)]
+    partners += [at_z(jnp.where(relays == 1, -base[0] - n, base[1] + n)) for n in range(PAIRS)]
     for partner in partners:
         pl.semaphore_signal(barrier, inc=1, device_id=partner, device_id_type=MESH)
 
-    one = lax.broadcasted_iota(jnp.int32, (rows, rows), 0) == lax.broadcasted_iota(jnp.int32, (rows, rows), 1)
-    one = one.astype(BF16)
-    ids_t = lax.dot_general(ids_ref[...].astype(F32).astype(BF16), one, TN, preferred_element_type=F32)
-    sc_t = lax.dot_general(sc_ref[...], one, TN, preferred_element_type=F32)
     msg[:, :feat] = og_ref[...]
-    msg[:, feat:] = jnp.concatenate([ids_t, sc_t], axis=1).astype(BF16)
+    msg[:, feat:] = jnp.concatenate([ids_ref[...].astype(F32), sc_ref[...].astype(F32)], axis=1).astype(BF16)
     yown[pl.ds(y, 1)] = og_ref[...][None]
     pl.semaphore_wait(barrier, len(partners))
 
@@ -78,67 +77,51 @@
             src_ref=src, dst_ref=dst, send_sem=send, recv_sem=recv, device_id=where, device_id_type=MESH
         )
 
-    def raw_first(way):
-        k = 6 - j if way == 0 else j + 3
+    def raw_first(way, far):
+        k = (8 if far else 6) - j if way == 0 else (5 if far else 3) + j
+        n = 3 - j if way == 0 else j
         return remote(
-            msg, raw.at[way, k], raw_send.at[way, 0], raw_recv.at[way, k], at_z(k if way == 0 else -k)
-        )
-
-    def raw_copy(way, s):
-        return remote(
-            raw.at[way, s - 1], raw.at[way, s], raw_send.at[way, s], raw_recv.at[way, s], at_z(1 - 2 * way)
-        )
-
-    def takes(way, s):
-        if s == 3:
-            return j == 2 - way, 0
-        if s == 4:
-            return (j >= 2, 3 - j) if way == 0 else (j <= 1, j)
-        if s == 5:
-            return (j != 1, (j == 2).astype(jnp.int32) + 1) if way == 0 else (j != 2, 2)
-        return True, {(0, 6): 3, (1, 6): 4, (0, 7): 5, (1, 7): 6, (0, 8): 7}[way, s]
-
-    def source(m):
-        if m == 0:
-            off = jnp.where(j == 0, 4, jnp.where(j == 1, 3, jnp.where(j == 2, -3, -4)))
-        elif m == 1:
-            off = jnp.where(j == 0, -5, jnp.where(j == 1, 4, jnp.where(j == 2, -4, -5)))
-        elif m == 2:
-            off = jnp.where(j == 2, -5, 5)
-        else:
-            off = {3: -6, 4: 6, 5: -7, 6: 7, 7: -8}[m]
-        return lax.rem(z + off + NZ, NZ)
-
-    def when(condition):
-        if condition is True:
-            return lambda body: body()
-        return pl.when(condition)
-
-    def raw_step(s):
-        for way in (0, 1):
-            if s > RAW[way]:
-                continue
-            condition, m = takes(way, s)
-
-            @when(condition)
+            msg, raw.at[way, n], raw_send.at[way, far], raw_recv.at[way, n], at_z(k if way == 0 else -k)
+        )
+
+    def raw_copy(way, n):
+        piece = raw.at[way, n]
+        return remote(piece, piece, raw_send.at[way, 2 + n], raw_recv.at[way, n], at_z(1 - 2 * way))
+
+    def hands_on(way):
+        return relays == 1 - way
+
+    def source(way, n):
+        return lax.rem(z + (-base[0] - n if way == 0 else base[1] + n) + NZ, NZ)
+
+    def raw_relay(n):
+        for way in (0, 1):
+
+            @pl.when(hands_on(way))
             def _():
-                raw_copy(way, s).wait_recv()
-                if s < RAW[way]:
-                    raw_copy(way, s + 1).start()
-                block = raw[way, s]
-                p, h = m // 2, m % 2
-                ypair[pl.ds(p, 1), pl.ds(y, 1), pl.ds(h, 1)] = block[:, :feat][None, None, None]
-                place_in(block[:, feat:].astype(F32), m)
-
-    def y_buf(p):
-        return yown if p == OWN else ypair.at[p]
+                raw_copy(way, n).wait_recv()
+                raw_copy(way, n).start()
+
+    def raw_take(n):
+        for way in (0, 1):
+
+            @pl.when(jnp.logical_not(hands_on(way)))
+            def _():
+                raw_copy(way, n).wait_recv()
+
+            block = raw[way, n]
+            ypair[n, pl.ds(y, 1), way] = block[:, :feat][None]
+            place_in(block[:, feat:].astype(F32), n, way)
+
+    def own_copy(k):
+        return remote(og_ref, yown.at[y], own_send.at[k], own_recv.at[k], at_y(k))
 
     def y_copy(p, way, s):
-        piece = y_buf(p).at[lax.rem(y + (1 - s if way == 0 else s - 1) + ny, ny)]
+        piece = ypair.at[p, lax.rem(y + (1 - s if way == 0 else s - 1) + ny, ny)]
         return remote(piece, piece, y_send.at[p, way, s], y_recv.at[p, way, s], at_y(1 - 2 * way))
 
     def y_arrive(p, way, s):
-        piece = y_buf(p).at[lax.rem(y + (-s if way == 0 else s) + ny, ny)]
+        piece = ypair.at[p, lax.rem(y + (-s if way == 0 else s) + ny, ny)]
         return remote(piece, piece, y_send.at[p, way, s], y_recv.at[p, way, s], at_y(1 - 2 * way))
 
     def y_step(p, s):
@@ -162,12 +145,12 @@
         placed = jnp.logical_and(slot == place_in_expert, pick > 0.5)
         return jnp.where(placed, 1.0, 0.0).astype(BF16), jnp.where(placed, weight, 0.0).astype(BF16)
 
-    def place_in(meta, m):
+    def place_in(meta, p, way):
         line = lax.broadcasted_iota(jnp.int32, (NX * Q, rows), 0)
         expert = (line // Q * TEAMS + (y * (NX * TEAMS) + team)).astype(F32)
         place, weighted = placing(meta, expert, lax.rem(line, Q).astype(F32))
-        pw_pair[pl.ds(m, 1), pl.ds(0, 1)] = place[None, None]
-        pw_pair[pl.ds(m, 1), pl.ds(1, 1)] = weighted[None, None]
+        pw_pair[p, way, 0] = place
+        pw_pair[p, way, 1] = weighted
 
     def xz_copy(p, k):
         to = lax.rem(x + k, NX)
@@ -177,7 +160,7 @@
         y_step(p, 5)
         for h in (0, 1):
             packs = jnp.dot(
-                pw_pair[2 * p + h, 0], ypair[p, :, h].reshape(rows, feat), preferred_element_type=F32
+                pw_pair[p, h, 0], ypair[p, :, h].reshape(rows, feat), preferred_element_type=F32
             ).astype(BF16)
             xpack[p, :, h] = packs.reshape(NX, Q, feat)
         for k in (2, 1, 3):
@@ -194,13 +177,17 @@
             packed.at[t, to], rbuf.at[z, t, x], xo_send.at[d + 1, k], xo_recv.at[d + 1, k], at_x(k)
         )
 
-    def pack_own():
-        y_step(OWN, 5)
+    def place_own():
         line = lax.broadcasted_iota(jnp.int32, (TEAMS * NX * Q, rows), 0)
         expert = lax.rem(line // Q, NX) * TEAMS + line // (NX * Q) + y * (NX * TEAMS)
         place, weighted = placing(msg[:, feat:].astype(F32), expert.astype(F32), lax.rem(line, Q).astype(F32))
-        pw_own[...] = weighted
-        packs = jnp.dot(place, yown[...].reshape(rows, feat), preferred_element_type=F32).astype(BF16)
+        pw_own[0] = place
+        pw_own[1] = weighted
+
+    def pack_own():
+        for k in range(1, ny):
+            own_copy(k).wait_recv()
+        packs = jnp.dot(pw_own[0], yown[...].reshape(rows, feat), preferred_element_type=F32).astype(BF16)
         packed[...] = packs.reshape(TEAMS, NX, Q, feat)
         for d in (1, -1, 0):
             for k in (2, 1, 3):
@@ -274,7 +261,7 @@
     def pairs_expert(n, first):
         def saved(ref):
             parts = [
-                ref[k, pl.ds(source(2 * p + h), 1)]
+                ref[k, pl.ds(source(h, p), 1)]
                 for p in (first, first + 1)
                 for k in range(NX)
                 for h in (0, 1)
@@ -282,7 +269,7 @@
             return jnp.concatenate(parts, axis=0).reshape(2 * NX * 2 * Q, -1).astype(F32)
 
         pgz[pl.ds(first, 2)] = expert_part(n, saved).reshape(2, NX, 2, Q, feat)
-        for p in (first + 1, first):
+        for p in (first, first + 1):
             for k in (2, 1, 3):
                 cz_copy(p, k).start()
             cbuf[p, pl.ds(x, 1)] = pgz[p, pl.ds(x, 1)]
@@ -367,7 +354,7 @@
             cz_copy(p, k).wait_recv()
         for h in (0, 1):
             token = lax.dot_general(
-                pw_pair[2 * p + h, 1], cbuf[p, :, h].reshape(NX * Q, feat), TN, preferred_element_type=F32
+                pw_pair[p, h, 1], cbuf[p, :, h].reshape(NX * Q, feat), TN, preferred_element_type=F32
             )
             tok[p, :, h] = token.astype(BF16).reshape(ny, Q, feat)
 
@@ -376,197 +363,187 @@
         for d in (1, -1, 0):
             for k in range(1, NX):
                 co_copy(d, k).wait_recv()
-        token = lax.dot_general(pw_own[...], ybuf[...].reshape(-1, feat), TN, preferred_element_type=F32)
+        token = lax.dot_general(pw_own[1], ybuf[...].reshape(-1, feat), TN, preferred_element_type=F32)
         tok_own[...] = token.astype(BF16).reshape(ny, Q, feat)
 
-    def r_bufs(p):
-        return (tok_own, yso) if p == OWN else (tok.at[p], ysr.at[p])
+    def last_copy(k):
+        return remote(
+            tok_own.at[lax.rem(y + k, ny)], ylast.at[k], last_send.at[k], last_recv.at[k], at_y(k)
+        )
 
     def r_target(p, way, s):
         left = y_steps(p)[way] + 1 - s
         return lax.rem(y + (left if way == 0 else -left) + ny, ny)
 
     def r_copy(p, way, s):
-        mine, sums = r_bufs(p)
-        src = mine.at[r_target(p, way, s)] if s == 1 else sums.at[way, s - 1]
-        return remote(src, sums.at[way, s], r_send.at[p, way, s], r_recv.at[p, way, s], at_y(1 - 2 * way))
+        src = tok.at[p, r_target(p, way, s)] if s == 1 else ysr.at[p, way, s - 1]
+        return remote(src, ysr.at[p, way, s], r_send.at[p, way, s], r_recv.at[p, way, s], at_y(1 - 2 * way))
 
     def r_step(p, s):
-        mine, sums = r_bufs(p)
         for way in (0, 1):
             steps = y_steps(p)[way]
             if 2 <= s <= steps + 1:
                 r_copy(p, way, s - 1).wait_recv()
             if s <= steps:
                 if s > 1:
-                    term = mine[pl.ds(r_target(p, way, s), 1)][0].astype(F32)
-                    sums[way, s - 1] = (sums[way, s - 1].astype(F32) + term).astype(BF16)
+                    term = tok[p, pl.ds(r_target(p, way, s), 1)][0].astype(F32)
+                    ysr[p, way, s - 1] = (ysr[p, way, s - 1].astype(F32) + term).astype(BF16)
                 r_copy(p, way, s).start()
 
-    def r_total(p):
+    def v_copy(way, n):
+        return remote(
+            vmid.at[way, n], vmid.at[way, n], v_send.at[way, n], v_recv.at[way, n], at_z(2 * way - 1)
+        )
+
+    def v_last(way, n):
+        far = 1 - j // 2 if way == 0 else j // 2
+        k = base[way] + n
+        return remote(
+            vmid.at[way, n], vfin.at[way, far], v_send.at[way, n], f_recv.at[way, far],
+            at_z(-k if way == 0 else k),
+        )
+
+    def v_came(way, far):
+        return remote(
+            vmid.at[way, 0], vfin.at[way, far], v_send.at[way, 0], f_recv.at[way, far], at_z(2 * way - 1)
+        )
+
+    def r_finish(p):
         r_step(p, 5)
-        mine, sums = r_bufs(p)
-        total = mine[pl.ds(y, 1)][0].astype(F32)
-        for way in (0, 1):
-            total = total + sums[way, y_steps(p)[way]].astype(F32)
-        return total
-
-    def r_finish(p):
-        rs[pl.ds(2 * p, 2)] = r_total(p)
-
-    def v_copy(way, s, first):
-        to, where = (0, s) if first else (s - 1, 1)
-        return remote(
-            zret.at[way, s], zret.at[way, to], v_send.at[way, s], v_recv.at[way, to],
-            at_z(-where if way == 0 else where),
-        )
-
-    def v_cases(way, s):
-        condition, _ = takes(way, s)
-        if s > 6:
-            return ((True, False),)
-        end = j == 2 - way
-        if s == 3:
-            return ((condition, True),)
-        rest = jnp.logical_not(end)
-        if condition is True:
-            return ((end, True), (rest, False))
-        return ((jnp.logical_and(condition, end), True), (jnp.logical_and(condition, rest), False))
-
-    def v_step(s, way):
-        condition, m = takes(way, s)
-
-        @when(condition)
-        def _():
-            total = rs[pl.ds(m, 1)][0]
-            if s < RAW[way]:
-                v_copy(way, s + 1, False).wait_recv()
-                total = total + zret[way, s].astype(F32)
-            zret[way, s] = total.astype(BF16)
-
-        for condition, first in v_cases(way, s):
-
-            @when(condition)
+        total = tok[p, pl.ds(y, 1)][0].astype(F32)
+        for way in (0, 1):
+            total = total + ysr[p, way, y_steps(p)[way]].astype(F32)
+        rs[p] = total
+        for way in (0, 1):
+
+            @pl.when(jnp.logical_not(hands_on(way)))
             def _():
-                v_copy(way, s, first).start()
-
-    y_step(OWN, 1)
-    raw_first(0).start()
-    raw_first(1).start()
-    raw_step(3)
-    y_step(OWN, 2)
-    raw_step(4)
-    y_step(OWN, 3)
-    raw_step(5)
+                vmid[way, p] = rs[p, way].astype(BF16)
+                v_copy(way, p).start()
+
+    def v_step(n):
+        for way in (0, 1):
+
+            @pl.when(hands_on(way))
+            def _():
+                v_copy(way, n).wait_recv()
+                vmid[way, n] = (rs[n, way] + vmid[way, n].astype(F32)).astype(BF16)
+                v_last(way, n).start()
+
+    for way in (0, 1):
+        raw_first(way, 0).start()
+        raw_first(way, 1).start()
+    for k in (4, 3, 5, 2, 6, 1, 7):
+        own_copy(k).start()
+    place_own()
+    for n in range(PAIRS):
+        raw_relay(n)
+    pack_own()
+    raw_take(0)
     y_step(0, 1)
-    y_step(OWN, 4)
-    raw_step(6)
+    raw_take(1)
     y_step(1, 1)
     y_step(0, 2)
-    pack_own()
-    raw_step(7)
-    y_step(2, 1)
-    y_step(1, 2)
-    y_step(0, 3)
     for d in (1, -1, 0):
         for k in range(1, NX):
             xo_copy(d, k).wait_recv()
     z_step(1)
-    raw_step(8)
+    raw_take(2)
+    y_step(2, 1)
+    y_step(1, 2)
+    y_step(0, 3)
+    raw_take(3)
     y_step(3, 1)
+    z_step(2)
     y_step(2, 2)
     y_step(1, 3)
     y_step(0, 4)
-    z_step(2)
     y_step(3, 2)
+    z_step(3)
     y_step(2, 3)
     y_step(1, 4)
     pack_pair(0)
-    z_step(3)
     y_step(3, 3)
+    z_step(4)
     y_step(2, 4)
     pack_pair(1)
-    z_step(4)
     y_step(3, 4)
-    pack_pair(2)
     for load in loads:
         load.wait()
     team_hidden(0, team)
     z_step(5)
+    pack_pair(2)
+    team_expert(0, team)
     pack_pair(3)
-    team_expert(0, team)
     z_step(6)
     beside = lax.rem(team + 3 - 2 * (j // 2), TEAMS)
     team_hidden(1, beside)
     pairs_hidden(2, 0)
     team_expert(1, beside)
     b_step(5)
+    pairs_expert(2, 0)
     pairs_hidden(3, 2)
-    pairs_expert(2, 0)
     b_step(4)
     pairs_expert(3, 2)
+    combine_pair(0)
+    r_step(0, 1)
     b_step(3)
+    combine_pair(1)
+    r_step(1, 1)
+    r_step(0, 2)
+    combine_pair(2)
+    r_step(2, 1)
+    r_step(1, 2)
+    b_step(2)
+    r_step(0, 3)
     combine_pair(3)
     r_step(3, 1)
-    combine_pair(2)
-    r_step(2, 1)
+    r_step(2, 2)
+    r_step(1, 3)
+    r_step(0, 4)
+    b_step(1)
     r_step(3, 2)
-    b_step(2)
-    combine_pair(1)
-    r_step(1, 1)
-    r_step(2, 2)
+    r_step(2, 3)
+    r_step(1, 4)
+    r_finish(0)
+    finish_tree()
     r_step(3, 3)
-    combine_pair(0)
-    r_step(0, 1)
-    r_step(1, 2)
-    r_step(2, 3)
+    r_step(2, 4)
+    r_finish(1)
+    v_step(0)
+    combine_own()
+    for k in (4, 3, 5, 2, 6, 1, 7):
+        last_copy(k).start()
     r_step(3, 4)
-    b_step(1)
+    r_finish(2)
+    v_step(1)
     r_finish(3)
-    v_step(8, 0)
-    v_step(7, 1)
-    r_step(0, 2)
-    r_step(1, 3)
-    r_step(2, 4)
-    finish_tree()
-    r_finish(2)
-    v_step(7, 0)
-    v_step(6, 1)
-    r_step(0, 3)
-    r_step(1, 4)
-    combine_own()
-    r_step(OWN, 1)
-    r_finish(1)
-    v_step(6, 0)
-    r_step(0, 4)
-    r_step(OWN, 2)
-    r_finish(0)
-    for s in (5, 4, 3):
-        for way in (0, 1):
-            v_step(s, way)
-        if s > 3:
-            r_step(OWN, 8 - s)
-    total = r_total(OWN)
+    v_step(2)
+    v_step(3)
+    total = tok_own[pl.ds(y, 1)][0].astype(F32)
+    for k in range(1, ny):
+        last_copy(k).wait_recv()
+        total = total + ylast[k].astype(F32)
     for way in (0, 1):
-        v_copy(way, 1, False).wait_recv()
-        total = total + zret[way, 0].astype(F32)
+        for far in (0, 1):
+            v_came(way, far).wait_recv()
+            total = total + vfin[way, far].astype(F32)
     out_ref[...] = total.astype(BF16)
 
+    for k in range(1, ny):
+        own_copy(k).wait_send()
+        last_copy(k).wait_send()
     for way in (0, 1):
-        raw_first(way).wait_send()
-        for s in range(3, RAW[way] + 1):
-            condition, _ = takes(way, s)
-            if s < RAW[way]:
-
-                @when(condition)
-                def _():
-                    raw_copy(way, s + 1).wait_send()
-
-            @when(condition)
+        for far in (0, 1):
+            raw_first(way, far).wait_send()
+        for n in range(PAIRS):
+
+            @pl.when(hands_on(way))
             def _():
-                v_copy(way, s, False).wait_send()
-
-        for p in range(PAIRS + 1):
+                raw_copy(way, n).wait_send()
+
+            v_copy(way, n).wait_send()
+        for p in range(PAIRS):
             for s in range(1, y_steps(p)[way] + 1):
                 y_copy(p, way, s).wait_send()
                 r_copy(p, way, s).wait_send()
@@ -619,11 +596,11 @@
             pltpu.VMEM((feat, hid), BF16),
             pltpu.VMEM((hid, feat), BF16),
             pltpu.VMEM((Q, feat + META), BF16),
-            pltpu.VMEM((2, RAW[0] + 1, Q, feat + META), BF16),
+            pltpu.VMEM((2, PAIRS, Q, feat + META), BF16),
             pltpu.VMEM((ny, Q, feat), BF16),
             pltpu.VMEM((PAIRS, ny, 2, Q, feat), BF16),
-            pltpu.VMEM((TEAMS * NX * Q, rows), BF16),
-            pltpu.VMEM((2 * PAIRS, 2, NX * Q, rows), BF16),
+            pltpu.VMEM((2, TEAMS * NX * Q, rows), BF16),
+            pltpu.VMEM((PAIRS, 2, 2, NX * Q, rows), BF16),
             pltpu.VMEM((TEAMS, NX, Q, feat), BF16),
             pltpu.VMEM((PAIRS, NX, 2, Q, feat), BF16),
             pltpu.VMEM((NZ, TEAMS, NX, Q, feat), BF16),
@@ -639,12 +616,14 @@
             pltpu.VMEM((PAIRS, ny, 2, Q, feat), BF16),
             pltpu.VMEM((ny, Q, feat), BF16),
             pltpu.VMEM((PAIRS, 2, 5, 2, Q, feat), BF16),
-            pltpu.VMEM((2, 5, Q, feat), BF16),
-            pltpu.VMEM((2 * PAIRS, Q, feat), F32),
-            pltpu.VMEM((2, RAW[0] + 1, Q, feat), BF16),
+            pltpu.VMEM((ny, Q, feat), BF16),
+            pltpu.VMEM((PAIRS, 2, Q, feat), F32),
+            pltpu.VMEM((2, PAIRS, Q, feat), BF16),
+            pltpu.VMEM((2, 2, Q, feat), BF16),
             pltpu.SemaphoreType.DMA((5,)),
-            *sems(2, RAW[0] + 1),
-            *sems(PAIRS + 1, 2, 5),
+            *sems(2, 2 + PAIRS),
+            *sems(ny),
+            *sems(PAIRS, 2, 5),
             *sems(3, NX),
             *sems(PAIRS, NX),
             *sems(2, FAR + 1, 2),
@@ -652,8 +631,10 @@
             *sems(2, FAR + 1, 2),
             *sems(3, NX),
             *sems(PAIRS, NX),
-            *sems(PAIRS + 1, 2, 5),
-            *sems(2, RAW[0] + 1),
+            *sems(PAIRS, 2, 5),
+            *sems(ny),
+            *sems(2, PAIRS),
+            *sems(2, 2),
         ],
         compiler_params=pltpu.CompilerParams(
             collective_id=0, has_side_effects=True, vmem_limit_bytes=56 * 1024 * 1024
@@ -661,8 +642,8 @@
         name="routed_backward",
     )(
         out_grad[0],
-        expert_ids[0],
-        gate_scores[0],
+        expert_ids[0].T,
+        gate_scores[0].T,
         saved_gate.reshape(saved_shape),
         saved_up.reshape(saved_shape),
         w_gate[0],

time: 130 us -> 121 us (0.931)
  Pallas kernels: 126 us -> 118 us
  local copies, waits for them, and re-layouts: 3.43 us -> 1.36 us
    pallas_call x1, Pallas kernels: 126 us -> 118 us  [per_device(): pl.pallas_call(functools.partial(kernel, ny), out_shape=jax.ShapeDtypeStr...]
    unnamed x7 -> x1, local copies, waits for them, and re-layouts: 3.43 us -> 1.36 us
where the time goes in v3:
time: 121 us; the launch traced here: 120 us
  Pallas kernels  118 us (98%)
  local copies, waits for them, and re-layouts  1.36 us (1%)
    pallas_call x1, Pallas kernels, per_device(): pl.pallas_call(functools.partial(kernel, ny), out_shape=jax.ShapeDtypeStr...  118 us

profile of v3, /device:TPU:6, one launch (start us, length us, event | category | flops | bytes accessed | tf_op | source)
XLA Modules:
  0.0 119.5 jit_solution(6606995582071795219)
XLA Ops:
  0.0 118.2 %routed_backward.1 = bf16[8,1792]{1,0:T(8,128)(2,1)} custom-call(bf16[8,1792]{1,0:T(8,128)(2,1)} %bitcast.19, s32[8,64]{1,0:T(8,128)} %bitcast.20, bf16[8,64]{1,0:T(8,128)(2,1)} %bitcast.21, bf16[4,16,8,256]{3,2,1,0:T(8,128)(2,1)} %bitcast.16, bf16[4,16,8,256]{3,2,1,0:T(8,128)(2,1)} %bitcast.17, bf16[1792,256]{1,0:T(8,128)(2,1)} %bitcast.13, ...), custom_call_target="tpu_custom_call" | custom-call | tf_op jit(solution)/shard_map/routed_backward/pallas_call | solution.py:587
  118.2 1.4 %copy.10 = bf16[1,8,1792]{2,1,0:T(8,128)(2,1)} copy(bf16[1,8,1792]{2,1,0:T(8,128)(2,1)} %bitcast.18) | data formatting | bytes 57344
